TPU v7x, 32 devices: a whole 2x2x4 slice. The times are simulated.
32 devices in a mesh: pipe: 8 (over z, x), dp: 4 (over y, core).
Axes of the slice: x: 2, y: 2, z: 4, core: 2. Of those that a mesh axis runs over, the one named last changes fastest.
Arguments:
- kept_down_first: bfloat16 [8, 256, 6144], P('pipe', 'dp'), may hold values from -6 to 6
- kept_up_first: bfloat16 [8, 256, 6144], P('pipe', 'dp'), may hold values from -6 to 6
- kept_down_second: bfloat16 [8, 256, 6144], P('pipe', 'dp'), may hold values from -6 to 6
- kept_up_second: bfloat16 [8, 256, 6144], P('pipe', 'dp'), may hold values from -6 to 6
- cot_down: bfloat16 [8, 256, 6144], P('pipe', 'dp'), may hold values from -6 to 6
- cot_up: bfloat16 [8, 256, 6144], P('pipe', 'dp'), may hold values from -6 to 6
- loss_down: bfloat16 [256, 6144], P('dp'), may hold values from -6 to 6
- loss_up: bfloat16 [256, 6144], P('dp'), may hold values from -6 to 6
- section_a: bfloat16 [8, 6144, 32], P('pipe')
- section_b: bfloat16 [8, 32, 6144], P('pipe')
- mirror_a: bfloat16 [8, 6144, 32], P('pipe'), as said below
- mirror_b: bfloat16 [8, 32, 6144], P('pipe')
Outputs:
- grad_a: float32 [8, 6144, 32], P('pipe', 'dp')
- grad_b: float32 [8, 32, 6144], P('pipe', None, 'dp')
Inputs may be any that keep to these rules, and one draw needn't show every extreme that they name: mirror_a[j] equals section_a[7-j] and mirror_b[j] equals section_b[7-j].
All inputs are finite; a program needn't handle non-finite values.
Results may differ from a plain program's by a relative error of at most 0.0051.
Values may be sent and summed in bfloat16 or wider, within the bound.
A program may use at most 64 MiB of HBM per device.

v0:
```python
import jax
import jax.numpy as jnp
from jax import lax
from jax.sharding import PartitionSpec as P

EPS = 1e-06


def swapped(value, axis, stride):
    mask = 2**stride
    pairs = [(source, source ^ mask) for source in range(lax.axis_size(axis))]
    return lax.ppermute(value, axis, pairs)


def passed_along(block, axis, distance):
    devices = range(lax.axis_size(axis))
    route = [(i - distance, i) for i in devices if i - distance in devices]
    return lax.ppermute(block, axis, route)


def section_back(inputs, grad_out, proj_a, proj_b):
    values = inputs.astype(jnp.float32)
    inverse = lax.rsqrt(jnp.mean(values * values, axis=-1, keepdims=True) + EPS)
    normed = values * inverse
    normed_b = normed.astype(jnp.bfloat16)
    pre = jnp.dot(normed_b, proj_a, preferred_element_type=jnp.float32)
    sigma = jax.nn.sigmoid(pre)
    hidden = (pre * sigma).astype(jnp.bfloat16)
    grad_b = jnp.dot(hidden.T, grad_out, preferred_element_type=jnp.float32)
    grad_hidden = jnp.dot(grad_out, proj_b.T, preferred_element_type=jnp.float32)
    grad_pre = (grad_hidden * sigma * (1.0 + pre * (1.0 - sigma))).astype(jnp.bfloat16)
    grad_a = jnp.dot(normed_b.T, grad_pre, preferred_element_type=jnp.float32)
    grad_norm = jnp.dot(grad_pre, proj_a.T, preferred_element_type=jnp.float32)
    inner = jnp.mean(grad_norm * normed, axis=-1, keepdims=True)
    grad_in = grad_out.astype(jnp.float32) + inverse * (grad_norm - normed * inner)
    return (grad_in.astype(jnp.bfloat16), grad_a, grad_b)


def mirror_move(moving, levels):
    for bit in range(levels):
        moving = swapped(moving, "pipe", bit)
    return moving


def per_device(
    kept_down_first,
    kept_up_first,
    kept_down_second,
    kept_up_second,
    cot_down,
    cot_up,
    loss_down,
    loss_up,
    section_a,
    section_b,
    mirror_a,
    mirror_b,
):
    position = lax.axis_index("pipe")
    sections = lax.axis_size("pipe")
    levels = sections.bit_length() - 1
    down_dx, down_a1, down_b1 = section_back(
        kept_down_first[0], cot_down[0], section_a[0], section_b[0]
    )
    up_dx, up_a1, up_b1 = section_back(kept_up_first[0], cot_up[0], mirror_a[0], mirror_b[0])
    from_above = passed_along(down_dx, "pipe", -1)
    from_below = passed_along(up_dx, "pipe", 1)
    second_down = jnp.where(position == sections - 1, loss_down, from_above)
    second_up = jnp.where(position == 0, loss_up, from_below)
    unused_d, down_a2, down_b2 = section_back(
        kept_down_second[0], second_down, section_a[0], section_b[0]
    )
    unused_u, up_a2, up_b2 = section_back(kept_up_second[0], second_up, mirror_a[0], mirror_b[0])
    own_a = down_a1 + down_a2
    own_b = down_b1 + down_b2
    other_a = up_a1 + up_a2
    other_b = up_b1 + up_b2
    factor = 1.0 / jnp.sqrt(jnp.float32(kept_down_first.shape[1] * lax.axis_size("dp")))
    split_at = other_a.size
    moving = jnp.concatenate([other_a.reshape(-1), other_b.reshape(-1)])
    moving = mirror_move(moving, levels)
    total_a = own_a + moving[:split_at].reshape(other_a.shape)
    total_b = own_b + moving[split_at:].reshape(other_b.shape)
    result_a, result_b = (
        lax.psum_scatter(total_a, "dp", scatter_dimension=0, tiled=True),
        lax.psum_scatter(total_b, "dp", scatter_dimension=1, tiled=True),
    )
    return ((result_a * factor)[None], (result_b * factor)[None])


def solution(mesh):
    placed = (
        P("pipe", "dp", None),
        P("pipe", "dp", None),
        P("pipe", "dp", None),
        P("pipe", "dp", None),
        P("pipe", "dp", None),
        P("pipe", "dp", None),
        P("dp", None),
        P("dp", None),
        P("pipe", None, None),
        P("pipe", None, None),
        P("pipe", None, None),
        P("pipe", None, None),
    )
    return jax.shard_map(
        per_device,
        mesh=mesh,
        in_specs=placed,
        out_specs=(P("pipe", "dp", None), P("pipe", None, "dp")),
        check_vma=False,
    )
```

profile of v0, /device:TPU:16, one launch (start us, length us, event | category | flops | bytes accessed | tf_op | source)
XLA Modules:
  0.0 263.5 jit_solution(7193792444177261098)
XLA Ops:
  7.3 1.5 fusion.29
  12.6 3.4 %collective-permute-start.1 = (bf16[64,6144]{1,0:T(8,128)(2,1)}, bf16[64,6144]{1,0:T(8,128)(2,1)}, u32[]{:S(2)}, u32[]{:S(2)}) collective-permute-start(bf16[64,6144]{1,0:T(8,128)(2,1)} %fusion.28), channel_id=1, source_target_pairs={{0,4},{4,8},{8,12},{12,16},{16,20},{20,24},{24,28},{1,5},{5,9},{9,... | collective-permute-start | bytes 2359304 | tf_op jit(solution)/shard_map/ppermute | solution.py:18
  18.3 2.0 fusion.61
  20.2 14.8 %collective-permute-done.1 = bf16[64,6144]{1,0:T(8,128)(2,1)} collective-permute-done((bf16[64,6144]{1,0:T(8,128)(2,1)}, bf16[64,6144]{1,0:T(8,128)(2,1)}, u32[]{:S(2)}, u32[]{:S(2)}) %collective-permute-start.1) | collective-permute-done | bytes 786464 | tf_op jit(solution)/shard_map/ppermute | solution.py:18
  35.0 2.9 %convolution_add_fusion = f32[6144,32]{0,1:T(8,128)} fusion(f32[6144,32]{0,1:T(8,128)S(1)} %fusion.59, bf16[1,64,6144]{2,1,0:T(8,128)(2,1)S(1)} %copy-done.5, f32[64]{0:T(128)} %copy-done.17, bf16[1,32,6144]{2,1,0:T(8,128)(2,1)} %param.23, bf16[64,6144]{1,0:T(8,128)(2,1)S(1)} %copy-done.6, bf16[64,6144]{1,0:T(8,128)(2,1)} %collective-permute-done.1, ...), kind=kOutput, calls=%fused_computation | convolution fusion | flops 52119552 | bytes 4333825 | tf_op jit(solution)/shard_map/dot_general | solution.py:32
  37.9 2.0 copy.14
  39.9 1.6 reshape.108
  41.4 1.7 fusion.34
  45.1 34.7 %collective-permute-done.2 = f32[393216]{0:T(1024)S(1)} collective-permute-done((f32[393216]{0:T(1024)S(1)}, f32[393216]{0:T(1024)S(1)}, u32[]{:S(2)}, u32[]{:S(2)}) %collective-permute-start.2) | collective-permute-done | bytes 1572896 | tf_op jit(solution)/shard_map/ppermute | solution.py:12
  79.7 1.6 collective-permute-start.3
  82.9 31.3 %collective-permute-done.3 = f32[393216]{0:T(1024)} collective-permute-done((f32[393216]{0:T(1024)S(1)}, f32[393216]{0:T(1024)}, u32[]{:S(2)}, u32[]{:S(2)}) %collective-permute-start.3) | collective-permute-done | bytes 1572896 | tf_op jit(solution)/shard_map/ppermute | solution.py:12
  115.7 4.8 %collective-permute-start = (bf16[64,6144]{1,0:T(8,128)(2,1)}, bf16[64,6144]{1,0:T(8,128)(2,1)}, u32[]{:S(2)}, u32[]{:S(2)}) collective-permute-start(bf16[64,6144]{1,0:T(8,128)(2,1)} %fusion.18), channel_id=1, source_target_pairs={{4,0},{8,4},{12,8},{16,12},{20,16},{24,20},{28,24},{5,1},{9,5},{13... | collective-permute-start | bytes 2359304 | tf_op jit(solution)/shard_map/ppermute | solution.py:18
  124.5 72.0 %collective-permute-done = bf16[64,6144]{1,0:T(8,128)(2,1)} collective-permute-done((bf16[64,6144]{1,0:T(8,128)(2,1)}, bf16[64,6144]{1,0:T(8,128)(2,1)}, u32[]{:S(2)}, u32[]{:S(2)}) %collective-permute-start) | collective-permute-done | bytes 786464 | tf_op jit(solution)/shard_map/ppermute | solution.py:18
  196.4 2.4 convolution_add_fusion.2
  198.8 2.4 fusion.107
  202.2 2.4 add.103
  205.0 2.9 %convolution_add_fusion.1 = f32[6144,32]{0,1:T(8,128)} fusion(f32[6144,32]{0,1:T(8,128)S(1)} %fusion.57, bf16[1,64,6144]{2,1,0:T(8,128)(2,1)S(1)} %copy-done.8, f32[64]{0:T(128)S(1)} %add_rsqrt_fusion.2, bf16[1,32,6144]{2,1,0:T(8,128)(2,1)} %param.21, bf16[64,6144]{1,0:T(8,128)(2,1)S(1)} %copy-done.7, bf16[64,6144]{1,0:T(8,128)(2,1)} %collective-permute-done, ...), kind=kOutput, calls=%fused_computation.1 | convolution fusion | flops 52119552 | bytes 4333825 | tf_op jit(solution)/shard_map/dot_general | solution.py:32
  207.8 1.8 slice.27
  209.6 1.9 copy.15
  211.5 2.3 add.101
  213.9 15.1 %reduce-scatter.5.cloned.1.call-done = f32[32,1536]{1,0:T(8,128)} async-done(((f32[32,6144]{1,0:T(8,128)}), f32[32,1536]{1,0:T(8,128)}) %reduce-scatter.5.cloned.1.call-update) | async-done | bytes 196624 | tf_op jit(solution)/shard_map/reduce_scatter | solution.py:86
  229.0 1.6 multiply_bitcast_fusion
  230.6 24.4 %reduce-scatter.3.cloned.1.call-done = f32[1536,32]{0,1:T(8,128)} async-done(((f32[6144,32]{0,1:T(8,128)}), f32[1536,32]{0,1:T(8,128)}) %reduce-scatter.3.cloned.1.call-update) | async-done | bytes 196624 | tf_op jit(solution)/shard_map/reduce_scatter | solution.py:85
  255.0 1.6 multiply_bitcast_fusion.1
  (68 shorter events, 16.3 us)
Async XLA Ops:
  7.2 1.6 copy-start
  7.2 3.6 %copy-start.1 = (bf16[1,64,6144]{2,1,0:T(8,128)(2,1)S(1)}, bf16[1,64,6144]{2,1,0:T(8,128)(2,1)}, u32[]{:S(2)}) copy-start(bf16[1,64,6144]{2,1,0:T(8,128)(2,1)} %param.13) | copy-start | bytes 2359300
  7.2 3.2 %copy-start.3 = (bf16[1,64,6144]{2,1,0:T(8,128)(2,1)S(1)}, bf16[1,64,6144]{2,1,0:T(8,128)(2,1)}, u32[]{:S(2)}) copy-start(bf16[1,64,6144]{2,1,0:T(8,128)(2,1)} %param.17) | copy-start | bytes 2359300
  7.2 3.2 %copy-start.10 = (bf16[1,32,6144]{2,1,0:T(8,128)(2,1)S(1)}, bf16[1,32,6144]{2,1,0:T(8,128)(2,1)}, u32[]{:S(2)}) copy-start(bf16[1,32,6144]{2,1,0:T(8,128)(2,1)} %param.23) | copy-start | bytes 1179652
  7.2 221.8 %reduce-scatter.5.cloned.1.call-start = ((), (), s32[]{:S(2)}) async-start(), calls=%async_computation.3 | async-start | bytes 983040 | tf_op jit(solution)/shard_map/reduce_scatter | solution.py:86
  10.4 0.9 copy-start.14
  11.2 4.8 %copy-start.5 = (bf16[1,64,6144]{2,1,0:T(8,128)(2,1)S(1)}, bf16[1,64,6144]{2,1,0:T(8,128)(2,1)}, u32[]{:S(2)}) copy-start(bf16[1,64,6144]{2,1,0:T(8,128)(2,1)} %param.15) | copy-start | bytes 2359300
  12.6 22.4 %collective-permute-start.1 = (bf16[64,6144]{1,0:T(8,128)(2,1)}, bf16[64,6144]{1,0:T(8,128)(2,1)}, u32[]{:S(2)}, u32[]{:S(2)}) collective-permute-start(bf16[64,6144]{1,0:T(8,128)(2,1)} %fusion.28), channel_id=1, source_target_pairs={{0,4},{4,8},{8,12},{12,16},{16,20},{20,24},{24,28},{1,5},{5,9},{9,... | collective-permute-start | bytes 2359304 | tf_op jit(solution)/shard_map/ppermute | solution.py:18
  18.2 16.8 %copy-start.6 = (bf16[64,6144]{1,0:T(8,128)(2,1)S(1)}, bf16[64,6144]{1,0:T(8,128)(2,1)}, u32[]{:S(2)}) copy-start(bf16[64,6144]{1,0:T(8,128)(2,1)} %param.19) | copy-start | bytes 2359300
  18.3 16.7 %copy-start.16 = (f32[64,32]{0,1:T(8,128)S(1)}, f32[64,32]{0,1:T(8,128)}, u32[]{:S(2)}) copy-start(f32[64,32]{0,1:T(8,128)} %fusion.44) | copy-start | bytes 24580
  43.1 1.1 copy-start.9
  44.3 37.0 %copy-start.2 = (bf16[1,64,6144]{2,1,0:T(8,128)(2,1)S(1)}, bf16[1,64,6144]{2,1,0:T(8,128)(2,1)}, u32[]{:S(2)}) copy-start(bf16[1,64,6144]{2,1,0:T(8,128)(2,1)} %param.12) | copy-start | bytes 2359300
  44.3 37.3 %copy-start.12 = (bf16[1,6144,32]{1,2,0:T(8,128)(2,1)S(1)}, bf16[1,6144,32]{1,2,0:T(8,128)(2,1)}, u32[]{:S(2)}) copy-start(bf16[1,6144,32]{1,2,0:T(8,128)(2,1)} %param.20) | copy-start | bytes 1179652
  44.4 37.6 %copy-start.4 = (bf16[1,64,6144]{2,1,0:T(8,128)(2,1)S(1)}, bf16[1,64,6144]{2,1,0:T(8,128)(2,1)}, u32[]{:S(2)}) copy-start(bf16[1,64,6144]{2,1,0:T(8,128)(2,1)} %param.16) | copy-start | bytes 2359300
  44.4 37.6 %copy-start.11 = (bf16[1,32,6144]{2,1,0:T(8,128)(2,1)S(1)}, bf16[1,32,6144]{2,1,0:T(8,128)(2,1)}, u32[]{:S(2)}) copy-start(bf16[1,32,6144]{2,1,0:T(8,128)(2,1)} %param.21) | copy-start | bytes 1179652
  44.4 35.3 %collective-permute-start.2 = (f32[393216]{0:T(1024)S(1)}, f32[393216]{0:T(1024)S(1)}, u32[]{:S(2)}, u32[]{:S(2)}) collective-permute-start(f32[393216]{0:T(1024)S(1)} %pad_maximum_fusion), channel_id=1, source_target_pairs={{0,4},{4,0},{8,12},{12,8},{16,20},{20,16},{24,28},{28,24},{1,5},{5... | collective-permute-start | bytes 4718600 | tf_op jit(solution)/shard_map/ppermute | solution.py:12
  79.7 34.5 %collective-permute-start.3 = (f32[393216]{0:T(1024)S(1)}, f32[393216]{0:T(1024)}, u32[]{:S(2)}, u32[]{:S(2)}) collective-permute-start(f32[393216]{0:T(1024)S(1)} %collective-permute-done.2), channel_id=1, source_target_pairs={{0,8},{4,12},{8,0},{12,4},{16,24},{20,28},{24,16},{28,20},{1,9},{5... | collective-permute-start | bytes 4718600 | tf_op jit(solution)/shard_map/ppermute | solution.py:12
  82.0 0.9 copy-start.15
  114.2 84.6 %collective-permute-start.4 = (f32[393216]{0:T(1024)}, f32[393216]{0:T(1024)}, u32[]{:S(2)}, u32[]{:S(2)}) collective-permute-start(f32[393216]{0:T(1024)} %collective-permute-done.3), channel_id=1, source_target_pairs={{0,16},{4,20},{8,24},{12,28},{16,0},{20,4},{24,8},{28,12},{1,17},{... | collective-permute-start | bytes 4718600 | tf_op jit(solution)/shard_map/ppermute | solution.py:12
  114.3 6.2 %copy-start.8 = (bf16[1,64,6144]{2,1,0:T(8,128)(2,1)S(1)}, bf16[1,64,6144]{2,1,0:T(8,128)(2,1)}, u32[]{:S(2)}) copy-start(bf16[1,64,6144]{2,1,0:T(8,128)(2,1)} %param.14) | copy-start | bytes 2359300
  115.7 80.7 %collective-permute-start = (bf16[64,6144]{1,0:T(8,128)(2,1)}, bf16[64,6144]{1,0:T(8,128)(2,1)}, u32[]{:S(2)}, u32[]{:S(2)}) collective-permute-start(bf16[64,6144]{1,0:T(8,128)(2,1)} %fusion.18), channel_id=1, source_target_pairs={{4,0},{8,4},{12,8},{16,12},{20,16},{24,20},{28,24},{5,1},{9,5},{13... | collective-permute-start | bytes 2359304 | tf_op jit(solution)/shard_map/ppermute | solution.py:18
  121.3 75.1 %copy-start.7 = (bf16[64,6144]{1,0:T(8,128)(2,1)S(1)}, bf16[64,6144]{1,0:T(8,128)(2,1)}, u32[]{:S(2)}) copy-start(bf16[64,6144]{1,0:T(8,128)(2,1)} %param.18) | copy-start | bytes 2359300
  123.4 75.4 %copy-start.13 = (f32[64,32]{0,1:T(8,128)}, f32[64,32]{0,1:T(8,128)S(1)}, u32[]{:S(2)}) copy-start(f32[64,32]{0,1:T(8,128)S(1)} %fusion.51) | copy-start | bytes 24580
  204.6 50.5 %reduce-scatter.3.cloned.1.call-start = ((), (), s32[]{:S(2)}) async-start(), calls=%async_computation.2 | async-start | bytes 983040 | tf_op jit(solution)/shard_map/reduce_scatter | solution.py:85
  (1 other events, 0.6 us)
Sparse Core Ops, SparseCore 0:
  204.7 24.3 reduce-scatter.4
  231.7 23.2 reduce-scatter.2
where the time goes:
time: 266 us; the launch traced here: 264 us
  waiting for transfers between devices  192 us (72%)
  matrix products  19.5 us (7%)
  other arithmetic  14.4 us (5%)
  between operations  14.3 us (5%)
  local copies, waits for them, and re-layouts  12.4 us (5%)
  starting transfers between devices  10.7 us (4%)
    ppermute x2, waiting for transfers between devices, passed_along(): return lax.ppermute(block, axis, route)  86.7 us
    ppermute x3, waiting for transfers between devices, swapped(): return lax.ppermute(value, axis, pairs)  66 us
    reduce_scatter x1, waiting for transfers between devices, per_device(): lax.psum_scatter(total_a, 'dp', scatter_dimension=0, tiled=True)  24.4 us
    reduce_scatter x1, waiting for transfers between devices, per_device(): lax.psum_scatter(total_b, 'dp', scatter_dimension=1, tiled=True)  15.1 us
    ppermute x2, starting transfers between devices, passed_along(): return lax.ppermute(block, axis, route)  8.18 us
    dot_general x4, matrix products, section_back(): grad_b = jnp.dot(hidden.T, grad_out, preferred_element_type=jnp.float32)  7.03 us
    dot_general x4, matrix products, section_back(): grad_a = jnp.dot(normed_b.T, grad_pre, preferred_element_type=jnp.float32)  6.46 us
  transfers between devices with their start and end apart: 7, of which 6 were waited for; matrix products, arithmetic and copies ran while one was open for 9% of the time, Pallas kernels for 0%

commit v1 on v0

v1 whole, which is shorter than its diff:
```python
import functools

import jax
import jax.numpy as jnp
from jax import lax
from jax.experimental import pallas as pl
from jax.experimental.pallas import tpu as pltpu
from jax.sharding import PartitionSpec as P

EPS = 1e-06
F32 = jnp.float32
BF16 = jnp.bfloat16


def dot_nt(a, b):
    return lax.dot_general(a, b, (((1,), (1,)), ((), ())), preferred_element_type=F32)


def dot_nn(a, b):
    return lax.dot_general(a, b, (((1,), (0,)), ((), ())), preferred_element_type=F32)


def dot_tn(a, b):
    return lax.dot_general(a, b, (((0,), (0,)), ((), ())), preferred_element_type=F32)


def kernel(
    n,
    m,
    kdf,
    kuf,
    kds,
    kus,
    cd,
    cu,
    ld,
    lu,
    sa,
    sb,
    ma,
    mb,
    ga,
    gb,
    x1,
    x2,
    g1,
    ls,
    wa,
    wb,
    nb,
    dxb,
    hs,
    hr,
    gs,
    gr,
    bp,
    br,
    b2,
    br2,
    ap,
    ar,
    a2,
    ar2,
    rs,
    rr,
    ms,
    mr,
    loc,
    snd,
    rcv,
):
    rows, width = x1.shape[1:]
    rank = wa.shape[1]
    chunk = width // m
    half = width // 2
    hm = m // 2
    tile = min(chunk, 768)
    tiles = width // tile
    per = chunk // tile
    factor = 1.0 / float(rows * m) ** 0.5

    j = lax.axis_index("pipe")
    d = lax.axis_index("dp")
    par = lax.rem(d, 2)
    kk = lax.div(d, 2)
    up = lax.rem(j + 1, n)
    down = lax.rem(j + n - 1, n)
    mirror = n - 1 - j
    pair = (j, d + 1 - 2 * par)
    ahead, behind, across = (up, d), (down, d), (mirror, d)

    def peer(q):
        return lax.rem(kk + q, hm)

    loads = {}
    for at, (src, dst) in enumerate(
        (
            (kds, x2.at[0]),
            (sa, wa.at[0]),
            (kus, x2.at[1]),
            (ma, wa.at[1]),
            (kdf, x1.at[0]),
            (cd, g1.at[0]),
            (sb, wb.at[0]),
            (kuf, x1.at[1]),
            (cu, g1.at[1]),
            (mb, wb.at[1]),
            (ld, ls.at[0]),
            (lu, ls.at[1]),
        )
    ):
        loads[at] = pltpu.make_async_copy(src, dst, loc.at[at])
        loads[at].start()

    barrier = pltpu.get_barrier_semaphore()
    greeted = [ahead, behind, across, pair]
    greeted += [(j, peer(q) * 2 + par) for q in range(1, hm)]
    for other in greeted:
        pl.semaphore_signal(
            barrier, inc=1, device_id=other, device_id_type=pl.DeviceIdType.MESH
        )
    pl.semaphore_wait(barrier, len(greeted))

    def send(slot, src, dst, target):
        copy = pltpu.make_async_remote_copy(
            src_ref=src,
            dst_ref=dst,
            send_sem=snd.at[slot],
            recv_sem=rcv.at[slot],
            device_id=target,
            device_id_type=pl.DeviceIdType.MESH,
        )
        copy.start()
        return copy

    mine = pl.ds(pl.multiple_of(par * half, 128), half)
    toward = (ahead, behind)
    back = (behind, ahead)
    halves = [
        send(w, src.at[:, mine], nb.at[w, par], toward[w])
        for w, src in enumerate((sb, mb))
    ]

    def cols(t):
        return pl.ds(pl.multiple_of(t * tile, 128), tile)

    def square_sum(x):
        xf = x.astype(F32)
        return jnp.sum(xf * xf, axis=-1, keepdims=True)

    zero_r = jnp.zeros((rows, rank), F32)
    zero_1 = jnp.zeros((rows, 1), F32)

    inverse2, pre2 = [], []
    hidden_copies = []
    for w in range(2):
        loads[2 * w].wait()
        loads[2 * w + 1].wait()

        def forward(t, carry, w=w):
            ss, xa = carry
            x = x2[w, :, cols(t)]
            return ss + square_sum(x), xa + dot_nt(x, wa[w, :, cols(t)])

        ss, xa = lax.fori_loop(0, tiles, forward, (zero_1, zero_r))
        inv = lax.rsqrt(ss / width + EPS)
        pre = xa * inv
        inverse2.append(inv)
        pre2.append(pre)
        h = pre * jax.nn.sigmoid(pre)
        hs[w] = jnp.concatenate([h] * (128 // rank), axis=1).astype(BF16)
        hidden_copies.append(send(4 + w, hs.at[w], hr.at[w], toward[w]))

    first = []
    for w in range(2):
        for at in range(3):
            loads[4 + 3 * w + at].wait()

        def project(t, carry, w=w):
            ss, xa, gh = carry
            x = x1[w, :, cols(t)]
            return (
                ss + square_sum(x),
                xa + dot_nt(x, wa[w, :, cols(t)]),
                gh + dot_nt(g1[w, :, cols(t)], wb[w, :, cols(t)]),
            )

        ss, xa, gh = lax.fori_loop(0, tiles, project, (zero_1, zero_r, zero_r))
        inv = lax.rsqrt(ss / width + EPS)
        pre = xa * inv
        sg = jax.nn.sigmoid(pre)
        h = (pre * sg).astype(BF16)
        dp = gh * sg * (1.0 + pre * (1.0 - sg))
        dpb = dp.astype(BF16)
        inner = jnp.sum(dpb.astype(F32) * pre, axis=-1, keepdims=True) / width
        first.append((inv, h, dpb, inv * inv * inner, (dp * inv).astype(BF16)))

    passed = []
    for w in range(2):
        halves[w].wait_recv()
        passed.append(send(2 + w, nb.at[w, par], nb.at[w, par], pair))
    loads[10].wait()
    loads[11].wait()
    edge = (j == 0, j == n - 1)

    returned = []
    for w in range(2):
        inv, h, dpb, scale, wdp = first[w]
        passed[w].wait_recv()

        def cotangent(t, gh, w=w, inv=inv, dpb=dpb, scale=scale):
            e = dot_nn(dpb, wa[w, :, cols(t)])
            dx = (
                g1[w, :, cols(t)].astype(F32)
                + inv * e
                - x1[w, :, cols(t)].astype(F32) * scale
            )
            dx = jnp.where(edge[w], ls[w, :, cols(t)].astype(F32), dx).astype(BF16)
            dxb[w, :, cols(t)] = dx
            side = lax.div(t, tiles // 2)
            at = lax.rem(t, tiles // 2)
            return gh + dot_nt(dx, nb[w, side, :, cols(at)])

        gh = lax.fori_loop(0, tiles, cotangent, zero_r)
        gs[w] = jnp.concatenate([gh] * (128 // rank), axis=1)
        returned.append(send(6 + w, gs.at[w], gr.at[w], back[w]))

    def place(t):
        k = lax.div(t, per)
        at = pl.ds(pl.multiple_of(lax.rem(t, per) * tile, 128), tile)
        return lax.rem(k, 2), lax.div(k, 2), at

    for w in range(2):
        hidden_copies[w].wait_recv()
        inv, h, dpb, scale, wdp = first[w]
        h_next = hr[w][:, :rank]

        def grads_b(t, carry, w=w, h=h, h_next=h_next):
            odd, k, at = place(t)
            bp[odd, k, w, :, at] = dot_tn(h, g1[w, :, cols(t)]).astype(BF16)
            bp[odd, k, 2 + w, :, at] = dot_tn(h_next, dxb[w, :, cols(t)]).astype(BF16)
            return carry

        lax.fori_loop(0, tiles, grads_b, 0)
    b_one = send(8, bp.at[1 - par], br, pair)

    for w in range(2):
        returned[w].wait_recv()
        gh = gr[w][:, :rank]
        pre = pre2[w]
        sg = jax.nn.sigmoid(pre)
        wdp2 = (gh * sg * (1.0 + pre * (1.0 - sg)) * inverse2[w]).astype(BF16)
        wdp1 = first[w][4]

        def grads_a(t, carry, w=w, wdp1=wdp1, wdp2=wdp2):
            odd, k, at = place(t)
            total = dot_tn(wdp1, x1[w, :, cols(t)]) + dot_tn(wdp2, x2[w, :, cols(t)])
            ap[odd, k, w, :, at] = total.astype(BF16)
            return carry

        lax.fori_loop(0, tiles, grads_a, 0)
    a_one = send(9, ap.at[1 - par], ar, pair)

    def added(part, other, total, k, items):
        def body(i, carry):
            total[k, i] = (part[par, k, i].astype(F32) + other[k, i].astype(F32)).astype(BF16)
            return carry

        lax.fori_loop(0, items, body, 0)

    b_one.wait_recv()
    b_two = []
    for q in range(1, hm):
        added(bp, br, b2, peer(q), 4)
        b_two.append(
            send(13 + q, b2.at[peer(q)], br2.at[q - 1], (j, peer(q) * 2 + par))
        )
    a_one.wait_recv()
    a_two = []
    for q in range(1, hm):
        added(ap, ar, a2, peer(q), 2)
        a_two.append(
            send(
                12 + hm + q, a2.at[peer(q)], ar2.at[q - 1], (j, peer(q) * 2 + par)
            )
        )

    def final(part, other, arrived, i):
        total = part[par, kk, i].astype(F32) + other[kk, i].astype(F32)
        for q in range(1, hm):
            total = total + arrived[q - 1, i].astype(F32)
        return total

    for copy in b_two:
        copy.wait_recv()
    rings = []
    for w in range(2):
        rs[w] = final(bp, br, br2, 2 + w).astype(BF16)
        rings.append(send(10 + w, rs.at[w], rr.at[w], back[w]))
    for copy in a_two:
        copy.wait_recv()
    ms[0] = final(ap, ar, ar2, 1).astype(BF16)
    mirror_a = send(12, ms.at[0], mr.at[0], across)
    rings[1].wait_recv()
    ms[1] = (final(bp, br, br2, 1) + rr[1].astype(F32)).astype(BF16)
    mirror_b = send(13, ms.at[1], mr.at[1], across)
    own_a = final(ap, ar, ar2, 0)
    ga[...] = own_a
    rings[0].wait_recv()
    gb[...] = final(bp, br, br2, 0) + rr[0].astype(F32)
    mirror_a.wait_recv()
    ga[...] = (ga[...] + mr[0].astype(F32)) * factor
    mirror_b.wait_recv()
    gb[...] = (gb[...] + mr[1].astype(F32)) * factor

    started = halves + passed + hidden_copies + returned + b_two + a_two + rings
    for copy in started + [b_one, a_one, mirror_a, mirror_b]:
        copy.wait_send()


def per_device(n, m, *args):
    flat = [a if a.ndim == 2 else a[0] for a in args]
    for at in (8, 10):
        flat[at] = flat[at].T
    rows, width = flat[0].shape
    rank = flat[8].shape[0]
    chunk = width // m
    hm = m // 2
    copies = 14 + 2 * (hm - 1)

    def vmem(*shape, dtype=BF16):
        return pltpu.VMEM(shape, dtype)

    grad_a, grad_b = pl.pallas_call(
        functools.partial(kernel, n, m),
        out_shape=[jax.ShapeDtypeStruct((rank, chunk), F32)] * 2,
        in_specs=[pl.BlockSpec(memory_space=pltpu.HBM)] * 12,
        out_specs=[pl.BlockSpec(memory_space=pltpu.VMEM)] * 2,
        scratch_shapes=[
            vmem(2, rows, width),
            vmem(2, rows, width),
            vmem(2, rows, width),
            vmem(2, rows, width),
            vmem(2, rank, width),
            vmem(2, rank, width),
            vmem(2, 2, rank, width // 2),
            vmem(2, rows, width),
            vmem(2, rows, 128),
            vmem(2, rows, 128),
            vmem(2, rows, 128, dtype=F32),
            vmem(2, rows, 128, dtype=F32),
            vmem(2, hm, 4, rank, chunk),
            vmem(hm, 4, rank, chunk),
            vmem(hm, 4, rank, chunk),
            vmem(hm - 1, 4, rank, chunk),
            vmem(2, hm, 2, rank, chunk),
            vmem(hm, 2, rank, chunk),
            vmem(hm, 2, rank, chunk),
            vmem(hm - 1, 2, rank, chunk),
            vmem(2, rank, chunk),
            vmem(2, rank, chunk),
            vmem(2, rank, chunk),
            vmem(2, rank, chunk),
            pltpu.SemaphoreType.DMA((12,)),
            pltpu.SemaphoreType.DMA((copies,)),
            pltpu.SemaphoreType.DMA((copies,)),
        ],
        compiler_params=pltpu.CompilerParams(
            collective_id=0, has_side_effects=True, vmem_limit_bytes=40 * 2**20
        ),
        name="relay_backward",
    )(*flat)
    return grad_a.T[None], grad_b[None]


def solution(mesh):
    n, m = mesh.shape["pipe"], mesh.shape["dp"]
    row, part = P("pipe", "dp", None), P("dp", None)
    table = P("pipe", None, None)
    return jax.shard_map(
        functools.partial(per_device, n, m),
        mesh=mesh,
        in_specs=(row,) * 6 + (part,) * 2 + (table,) * 4,
        out_specs=(P("pipe", "dp", None), P("pipe", None, "dp")),
        check_vma=False,
    )
```

time: 266 us -> 68.3 us (0.26)
  waiting for transfers between devices: 192 us -> 0 us
  Pallas kernels: 0 us -> 52.7 us
  matrix products: 19.5 us -> 0 us
  other arithmetic: 14.4 us -> 0 us
  between operations: 14.3 us -> 0.66 us
  starting transfers between devices: 10.7 us -> 0 us
    ppermute x5 -> x0, waiting for transfers between devices: 153 us -> none  [the longest x2 86.7 us: passed_along(): return lax.ppermute(block, axis, route)]
    pallas_call x0 -> x1, Pallas kernels: none -> 52.7 us  [per_device(): pl.pallas_call(functools.partial(kernel, n, m), out_shape=[jax.ShapeDtype...]
    reduce_scatter x2 -> x0, waiting for transfers between devices: 39.5 us -> none  [the longest x1 24.4 us: per_device(): lax.psum_scatter(total_a, 'dp', scatter_dimension=0, tiled=True)]
    dot_general x16 -> x0, matrix products: 19.5 us -> none  [the longest x4 7.03 us: section_back(): grad_b = jnp.dot(hidden.T, grad_out, preferred_element_type=jnp.float32)]
    unnamed x37 -> x26, local copies, waits for them, and re-layouts: 1.82 us -> 14.4 us
    ppermute x5 -> x0, starting transfers between devices: 10.6 us -> none  [the longest x2 8.18 us: passed_along(): return lax.ppermute(block, axis, route)]
    slice x4 -> x0, local copies, waits for them, and re-layouts: 7.04 us -> none  [the longest x2 3.69 us: per_device(): total_a = own_a + moving[:split_at].reshape(other_a.shape)]
    add x2 -> x0, other arithmetic: 4.71 us -> none  [the longest x1 2.36 us: per_device(): total_b = own_b + moving[split_at:].reshape(other_b.shape)]
  transfers between devices with their start and end apart: 7 -> 0, of which waited for: 6 -> 0; matrix products, arithmetic and copies ran while one was open for 9% -> 0% of each run, Pallas kernels for 0% -> 0%
where the time goes in v1:
time: 68.3 us; the launch traced here: 67.7 us
  Pallas kernels  52.7 us (77%)
  local copies, waits for them, and re-layouts  14.4 us (21%)
    pallas_call x1, Pallas kernels, per_device(): pl.pallas_call(functools.partial(kernel, n, m), out_shape=[jax.ShapeDtype...  52.7 us
    unnamed x26, local copies, waits for them, and re-layouts  14.4 us

profile of v1, /device:TPU:16, one launch (start us, length us, event | category | flops | bytes accessed | tf_op | source)
XLA Modules:
  0.0 67.7 jit_solution(17417460634198128143)
XLA Ops:
  0.6 0.0 copy-start
  0.6 1.1 %copy-done = bf16[1,64,6144]{2,1,0:T(8,128)(2,1)S(1)} copy-done((bf16[1,64,6144]{2,1,0:T(8,128)(2,1)S(1)}, bf16[1,64,6144]{2,1,0:T(8,128)(2,1)}, u32[]{:S(2)}) %copy-start) | copy-done | bytes 786456
  1.8 0.0 copy-start.1
  1.8 1.1 %copy-done.1 = bf16[1,64,6144]{2,1,0:T(8,128)(2,1)S(1)} copy-done((bf16[1,64,6144]{2,1,0:T(8,128)(2,1)S(1)}, bf16[1,64,6144]{2,1,0:T(8,128)(2,1)}, u32[]{:S(2)}) %copy-start.1) | copy-done | bytes 786456
  2.9 0.0 copy-start.2
  2.9 1.1 %copy-done.2 = bf16[1,64,6144]{2,1,0:T(8,128)(2,1)S(1)} copy-done((bf16[1,64,6144]{2,1,0:T(8,128)(2,1)S(1)}, bf16[1,64,6144]{2,1,0:T(8,128)(2,1)}, u32[]{:S(2)}) %copy-start.2) | copy-done | bytes 786456
  4.0 0.0 copy-start.3
  4.0 1.1 %copy-done.3 = bf16[1,64,6144]{2,1,0:T(8,128)(2,1)S(1)} copy-done((bf16[1,64,6144]{2,1,0:T(8,128)(2,1)S(1)}, bf16[1,64,6144]{2,1,0:T(8,128)(2,1)}, u32[]{:S(2)}) %copy-start.3) | copy-done | bytes 786456
  5.2 0.0 copy-start.4
  5.2 1.1 %copy-done.4 = bf16[1,64,6144]{2,1,0:T(8,128)(2,1)S(1)} copy-done((bf16[1,64,6144]{2,1,0:T(8,128)(2,1)S(1)}, bf16[1,64,6144]{2,1,0:T(8,128)(2,1)}, u32[]{:S(2)}) %copy-start.4) | copy-done | bytes 786456
  6.3 0.0 copy-start.5
  6.3 1.1 %copy-done.5 = bf16[1,64,6144]{2,1,0:T(8,128)(2,1)S(1)} copy-done((bf16[1,64,6144]{2,1,0:T(8,128)(2,1)S(1)}, bf16[1,64,6144]{2,1,0:T(8,128)(2,1)}, u32[]{:S(2)}) %copy-start.5) | copy-done | bytes 786456
  7.4 0.0 copy-start.6
  7.4 1.1 %copy-done.6 = bf16[64,6144]{1,0:T(8,128)(2,1)S(1)} copy-done((bf16[64,6144]{1,0:T(8,128)(2,1)S(1)}, bf16[64,6144]{1,0:T(8,128)(2,1)}, u32[]{:S(2)}) %copy-start.6) | copy-done | bytes 786456
  8.6 0.0 copy-start.7
  8.6 1.1 %copy-done.7 = bf16[64,6144]{1,0:T(8,128)(2,1)S(1)} copy-done((bf16[64,6144]{1,0:T(8,128)(2,1)S(1)}, bf16[64,6144]{1,0:T(8,128)(2,1)}, u32[]{:S(2)}) %copy-start.7) | copy-done | bytes 786456
  9.7 0.0 copy-start.8
  9.7 1.0 %copy-done.8 = bf16[1,6144,32]{1,2,0:T(8,128)(2,1)S(1)} copy-done((bf16[1,6144,32]{1,2,0:T(8,128)(2,1)S(1)}, bf16[1,6144,32]{1,2,0:T(8,128)(2,1)}, u32[]{:S(2)}) %copy-start.8) | copy-done | bytes 393240
  10.7 1.0 %copy-done.9 = bf16[1,32,6144]{2,1,0:T(8,128)(2,1)S(1)} copy-done((bf16[1,32,6144]{2,1,0:T(8,128)(2,1)S(1)}, bf16[1,32,6144]{2,1,0:T(8,128)(2,1)}, u32[]{:S(2)}) %copy-start.9) | copy-done | bytes 393240
  11.7 1.0 %copy-done.10 = bf16[1,6144,32]{1,2,0:T(8,128)(2,1)S(1)} copy-done((bf16[1,6144,32]{1,2,0:T(8,128)(2,1)S(1)}, bf16[1,6144,32]{1,2,0:T(8,128)(2,1)}, u32[]{:S(2)}) %copy-start.10) | copy-done | bytes 393240
  12.7 1.0 %copy-done.11 = bf16[1,32,6144]{2,1,0:T(8,128)(2,1)S(1)} copy-done((bf16[1,32,6144]{2,1,0:T(8,128)(2,1)S(1)}, bf16[1,32,6144]{2,1,0:T(8,128)(2,1)}, u32[]{:S(2)}) %copy-start.11) | copy-done | bytes 393240
  13.7 52.7 %relay_backward.1 = (f32[32,1536]{1,0:T(8,128)S(1)}, f32[32,1536]{1,0:T(8,128)S(1)}) custom-call(bf16[64,6144]{1,0:T(8,128)(2,1)S(1)} %bitcast.18, bf16[64,6144]{1,0:T(8,128)(2,1)S(1)} %bitcast.19, bf16[64,6144]{1,0:T(8,128)(2,1)S(1)} %bitcast.20, bf16[64,6144]{1,0:T(8,128)(2,1)S(1)} %bitcast.21, bf16[64,6144]{1,0:T(8,128)(2,1)S(1)} %bitcast.22, ...), custom_call_target="tpu_custom_call" | custom-call | tf_op jit(solution)/shard_map/relay_backward/pallas_call | solution.py:334
  66.3 0.7 %copy.16 = f32[1,1536,32]{1,2,0:T(8,128)} copy(f32[1,1536,32]{1,2,0:T(8,128)S(1)} %bitcast.29) | data formatting | bytes 393216
  67.0 0.7 copy.17
  (3 shorter events, 0.0 us)
Async XLA Ops:
  0.6 1.1 %copy-start = (bf16[1,64,6144]{2,1,0:T(8,128)(2,1)S(1)}, bf16[1,64,6144]{2,1,0:T(8,128)(2,1)}, u32[]{:S(2)}) copy-start(bf16[1,64,6144]{2,1,0:T(8,128)(2,1)} %param.12) | copy-start | bytes 2359300
  1.8 1.1 %copy-start.1 = (bf16[1,64,6144]{2,1,0:T(8,128)(2,1)S(1)}, bf16[1,64,6144]{2,1,0:T(8,128)(2,1)}, u32[]{:S(2)}) copy-start(bf16[1,64,6144]{2,1,0:T(8,128)(2,1)} %param.13) | copy-start | bytes 2359300
  2.9 1.1 %copy-start.2 = (bf16[1,64,6144]{2,1,0:T(8,128)(2,1)S(1)}, bf16[1,64,6144]{2,1,0:T(8,128)(2,1)}, u32[]{:S(2)}) copy-start(bf16[1,64,6144]{2,1,0:T(8,128)(2,1)} %param.14) | copy-start | bytes 2359300
  4.0 1.1 %copy-start.3 = (bf16[1,64,6144]{2,1,0:T(8,128)(2,1)S(1)}, bf16[1,64,6144]{2,1,0:T(8,128)(2,1)}, u32[]{:S(2)}) copy-start(bf16[1,64,6144]{2,1,0:T(8,128)(2,1)} %param.15) | copy-start | bytes 2359300
  5.2 1.1 %copy-start.4 = (bf16[1,64,6144]{2,1,0:T(8,128)(2,1)S(1)}, bf16[1,64,6144]{2,1,0:T(8,128)(2,1)}, u32[]{:S(2)}) copy-start(bf16[1,64,6144]{2,1,0:T(8,128)(2,1)} %param.16) | copy-start | bytes 2359300
  6.3 1.1 %copy-start.5 = (bf16[1,64,6144]{2,1,0:T(8,128)(2,1)S(1)}, bf16[1,64,6144]{2,1,0:T(8,128)(2,1)}, u32[]{:S(2)}) copy-start(bf16[1,64,6144]{2,1,0:T(8,128)(2,1)} %param.17) | copy-start | bytes 2359300
  7.4 1.1 %copy-start.6 = (bf16[64,6144]{1,0:T(8,128)(2,1)S(1)}, bf16[64,6144]{1,0:T(8,128)(2,1)}, u32[]{:S(2)}) copy-start(bf16[64,6144]{1,0:T(8,128)(2,1)} %ld.1) | copy-start | bytes 2359300
  8.6 1.1 %copy-start.7 = (bf16[64,6144]{1,0:T(8,128)(2,1)S(1)}, bf16[64,6144]{1,0:T(8,128)(2,1)}, u32[]{:S(2)}) copy-start(bf16[64,6144]{1,0:T(8,128)(2,1)} %lu.1) | copy-start | bytes 2359300
  9.7 1.0 %copy-start.8 = (bf16[1,6144,32]{1,2,0:T(8,128)(2,1)S(1)}, bf16[1,6144,32]{1,2,0:T(8,128)(2,1)}, u32[]{:S(2)}) copy-start(bf16[1,6144,32]{1,2,0:T(8,128)(2,1)} %param.20) | copy-start | bytes 1179652
  10.7 1.0 %copy-start.9 = (bf16[1,32,6144]{2,1,0:T(8,128)(2,1)S(1)}, bf16[1,32,6144]{2,1,0:T(8,128)(2,1)}, u32[]{:S(2)}) copy-start(bf16[1,32,6144]{2,1,0:T(8,128)(2,1)} %param.21) | copy-start | bytes 1179652
  11.7 1.0 %copy-start.10 = (bf16[1,6144,32]{1,2,0:T(8,128)(2,1)S(1)}, bf16[1,6144,32]{1,2,0:T(8,128)(2,1)}, u32[]{:S(2)}) copy-start(bf16[1,6144,32]{1,2,0:T(8,128)(2,1)} %param.22) | copy-start | bytes 1179652
  12.7 1.0 %copy-start.11 = (bf16[1,32,6144]{2,1,0:T(8,128)(2,1)S(1)}, bf16[1,32,6144]{2,1,0:T(8,128)(2,1)}, u32[]{:S(2)}) copy-start(bf16[1,32,6144]{2,1,0:T(8,128)(2,1)} %param.23) | copy-start | bytes 1179652

commit v2 on v1

v2 whole, which is shorter than its diff:
```python
import functools

import jax
import jax.numpy as jnp
from jax import lax
from jax.experimental import pallas as pl
from jax.experimental.pallas import tpu as pltpu
from jax.sharding import PartitionSpec as P

EPS = 1e-06
F32 = jnp.float32
BF16 = jnp.bfloat16


def dot_nt(a, b):
    return lax.dot_general(a, b, (((1,), (1,)), ((), ())), preferred_element_type=F32)


def dot_nn(a, b):
    return lax.dot_general(a, b, (((1,), (0,)), ((), ())), preferred_element_type=F32)


def dot_tn(a, b):
    return lax.dot_general(a, b, (((0,), (0,)), ((), ())), preferred_element_type=F32)


def kernel(
    n,
    m,
    kdf,
    kuf,
    kds,
    kus,
    cd,
    cu,
    ld,
    lu,
    sa,
    sb,
    ma,
    mb,
    ga,
    gb,
    x1,
    x2,
    g1,
    ls,
    wa,
    wb,
    nb,
    dxb,
    hs,
    hr,
    gs,
    gr,
    part,
    other,
    total,
    arrived,
    rs,
    rr,
    ms,
    mr,
    loc,
    snd,
    rcv,
):
    rows, width = x1.shape[1:]
    rank = wa.shape[1]
    chunk = width // m
    half = width // 2
    hm = m // 2
    tile = min(chunk, 768)
    tiles = width // tile
    per = chunk // tile
    factor = 1.0 / float(rows * m) ** 0.5

    j = lax.axis_index("pipe")
    d = lax.axis_index("dp")
    par = lax.rem(d, 2)
    kk = lax.div(d, 2)
    up = lax.rem(j + 1, n)
    down = lax.rem(j + n - 1, n)
    mirror = n - 1 - j
    pair = (j, d + 1 - 2 * par)
    ahead, behind, across = (up, d), (down, d), (mirror, d)

    def peer(q):
        return lax.rem(kk + q, hm)

    sources = (
        (kds, x2.at[0]),
        (sa, wa.at[0]),
        (kus, x2.at[1]),
        (ma, wa.at[1]),
        (kdf, x1.at[0]),
        (cd, g1.at[0]),
        (sb, wb.at[0]),
        (kuf, x1.at[1]),
        (cu, g1.at[1]),
        (mb, wb.at[1]),
    )
    loads = [
        pltpu.make_async_copy(src, dst, loc.at[at])
        for at, (src, dst) in enumerate(sources)
    ]

    barrier = pltpu.get_barrier_semaphore()
    greeted = [ahead, behind, across, pair]
    greeted += [(j, peer(q) * 2 + par) for q in range(1, hm)]
    for friend in greeted:
        pl.semaphore_signal(
            barrier, inc=1, device_id=friend, device_id_type=pl.DeviceIdType.MESH
        )
    for at in range(4):
        loads[at].start()
    pl.semaphore_wait(barrier, len(greeted))

    def send(slot, src, dst, target):
        copy = pltpu.make_async_remote_copy(
            src_ref=src,
            dst_ref=dst,
            send_sem=snd.at[slot],
            recv_sem=rcv.at[slot],
            device_id=target,
            device_id_type=pl.DeviceIdType.MESH,
        )
        copy.start()
        return copy

    mine = pl.ds(pl.multiple_of(par * half, 128), half)
    toward = (ahead, behind)
    back = (behind, ahead)
    halves = [
        send(w, src.at[:, mine], nb.at[w, par], toward[w])
        for w, src in enumerate((sb, mb))
    ]

    for at in range(4, 10):
        loads[at].start()
    edge = (j == 0, j == n - 1)
    losses = [
        pltpu.make_async_copy(src, ls, loc.at[10 + w]) for w, src in enumerate((ld, lu))
    ]
    for w in range(2):
        pl.when(edge[w])(losses[w].start)

    def cols(t):
        return pl.ds(pl.multiple_of(t * tile, 128), tile)

    def square_sum(x):
        xf = x.astype(F32)
        return jnp.sum(xf * xf, axis=-1, keepdims=True)

    def wide(x):
        return jnp.concatenate([x] * (128 // rank), axis=1)

    both = (0, 1)
    zero_r = jnp.zeros((rows, rank), F32)
    zero_1 = jnp.zeros((rows, 1), F32)

    def loop(body, start=0):
        return lax.fori_loop(0, tiles, body, start, unroll=2)

    for at in range(4):
        loads[at].wait()

    def forward(t, carry):
        after = []
        for w in both:
            ss, xa = carry[w]
            x = x2[w, :, cols(t)]
            after.append((ss + square_sum(x), xa + dot_nt(x, wa[w, :, cols(t)])))
        return tuple(after)

    inverse2, pre2 = [], []
    hidden_copies = []
    for w, (ss, xa) in enumerate(loop(forward, ((zero_1, zero_r),) * 2)):
        inv = lax.rsqrt(ss / width + EPS)
        pre = xa * inv
        inverse2.append(inv)
        pre2.append(pre)
        hs[w] = wide(pre * jax.nn.sigmoid(pre)).astype(BF16)
        hidden_copies.append(send(4 + w, hs.at[w], hr.at[w], toward[w]))

    for at in range(4, 10):
        loads[at].wait()

    def project(t, carry):
        after = []
        for w in both:
            ss, xa, gh = carry[w]
            x = x1[w, :, cols(t)]
            after.append(
                (
                    ss + square_sum(x),
                    xa + dot_nt(x, wa[w, :, cols(t)]),
                    gh + dot_nt(g1[w, :, cols(t)], wb[w, :, cols(t)]),
                )
            )
        return tuple(after)

    first = []
    for ss, xa, gh in loop(project, ((zero_1, zero_r, zero_r),) * 2):
        inv = lax.rsqrt(ss / width + EPS)
        pre = xa * inv
        sg = jax.nn.sigmoid(pre)
        h = (pre * sg).astype(BF16)
        dp = gh * sg * (1.0 + pre * (1.0 - sg))
        dpb = dp.astype(BF16)
        inner = jnp.sum(dpb.astype(F32) * pre, axis=-1, keepdims=True) / width
        first.append((inv, h, dpb, inv * inv * inner, (dp * inv).astype(BF16)))

    def place(t):
        k = lax.div(t, per)
        at = pl.ds(pl.multiple_of(lax.rem(t, per) * tile, 128), tile)
        return lax.rem(k, 2), lax.div(k, 2), at

    def send_half(g):
        return send(8 + g, part.at[g, 1 - par], other.at[g], pair)

    def send_quarters(g, copy):
        copy.wait_recv()
        copies = []
        for q in range(1, hm):
            k = peer(q)
            for i in range(2):
                total[g, k, i] = (
                    part[g, par, k, i].astype(F32) + other[g, k, i].astype(F32)
                ).astype(BF16)
            copies.append(
                send(
                    14 + g * (hm - 1) + q,
                    total.at[g, k],
                    arrived.at[g, q - 1],
                    (j, k * 2 + par),
                )
            )
        return copies

    def final(g, i):
        value = part[g, par, kk, i].astype(F32) + other[g, kk, i].astype(F32)
        for q in range(1, hm):
            value = value + arrived[g, q - 1, i].astype(F32)
        return value

    def grads_first(t, carry):
        odd, k, at = place(t)
        for w in both:
            value = dot_tn(first[w][1], g1[w, :, cols(t)])
            part[0, odd, k, w, :, at] = value.astype(BF16)
        return carry

    loop(grads_first)
    half_first = send_half(0)

    def cotangent(t, carry):
        for w in both:
            inv, h, dpb, scale, wdp = first[w]
            dx = (
                g1[w, :, cols(t)].astype(F32)
                + inv * dot_nn(dpb, wa[w, :, cols(t)])
                - x1[w, :, cols(t)].astype(F32) * scale
            )
            dxb[w, :, cols(t)] = dx.astype(BF16)
        return carry

    loop(cotangent)
    for w in both:

        @pl.when(edge[w])
        def _(w=w):
            losses[w].wait()

            def loss(t, carry):
                dxb[w, :, cols(t)] = ls[:, cols(t)]
                return carry

            lax.fori_loop(0, tiles, loss, 0)

    quarters = [send_quarters(0, half_first)]

    for copy in hidden_copies:
        copy.wait_recv()
    h_next = [hr[w][:, :rank] for w in both]

    def grads_second(t, carry):
        odd, k, at = place(t)
        for w in both:
            value = dot_tn(h_next[w], dxb[w, :, cols(t)])
            part[1, odd, k, w, :, at] = value.astype(BF16)
        return carry

    loop(grads_second)
    half_second = send_half(1)

    passed = []
    for w in both:
        halves[w].wait_recv()
        passed.append(send(2 + w, nb.at[w, par], nb.at[w, par], pair))
    quarters.append(send_quarters(1, half_second))

    for copy in passed:
        copy.wait_recv()

    def product(t, carry):
        side = lax.div(t, tiles // 2)
        at = cols(lax.rem(t, tiles // 2))
        return tuple(
            carry[w] + dot_nt(dxb[w, :, cols(t)], nb[w, side, :, at]) for w in both
        )

    returned = []
    for w, gh in enumerate(loop(product, (zero_r, zero_r))):
        gs[w] = wide(gh)
        returned.append(send(6 + w, gs.at[w], gr.at[w], back[w]))

    wdp2 = []
    for w in both:
        returned[w].wait_recv()
        pre = pre2[w]
        sg = jax.nn.sigmoid(pre)
        dp = gr[w][:, :rank] * sg * (1.0 + pre * (1.0 - sg))
        wdp2.append((dp * inverse2[w]).astype(BF16))

    def grads_a(t, carry):
        odd, k, at = place(t)
        for w in both:
            value = dot_tn(first[w][4], x1[w, :, cols(t)])
            value = value + dot_tn(wdp2[w], x2[w, :, cols(t)])
            part[2, odd, k, w, :, at] = value.astype(BF16)
        return carry

    loop(grads_a)
    half_a = send_half(2)

    quarters.append(send_quarters(2, half_a))

    for copy in quarters[1]:
        copy.wait_recv()
    rings = []
    for w in (1, 0):
        rs[w] = final(1, w).astype(BF16)
        rings.append(send(11 + w, rs.at[w], rr.at[w], back[w]))
    for copy in quarters[0]:
        copy.wait_recv()
    rings[0].wait_recv()
    ms[1] = (final(0, 1) + rr[1].astype(F32)).astype(BF16)
    mirror_b = send(14, ms.at[1], mr.at[1], across)
    for copy in quarters[2]:
        copy.wait_recv()
    ms[0] = final(2, 1).astype(BF16)
    mirror_a = send(13, ms.at[0], mr.at[0], across)
    rings[1].wait_recv()
    gb[...] = final(0, 0) + rr[0].astype(F32)
    ga[...] = final(2, 0)
    mirror_b.wait_recv()
    gb[...] = (gb[...] + mr[1].astype(F32)) * factor
    mirror_a.wait_recv()
    ga[...] = (ga[...] + mr[0].astype(F32)) * factor

    started = halves + passed + hidden_copies + returned + rings
    started += quarters[0] + quarters[1] + quarters[2]
    for copy in started + [half_first, half_second, half_a, mirror_a, mirror_b]:
        copy.wait_send()


def per_device(n, m, *args):
    flat = [a if a.ndim == 2 else a[0] for a in args]
    for at in (8, 10):
        flat[at] = flat[at].T
    rows, width = flat[0].shape
    rank = flat[8].shape[0]
    chunk = width // m
    hm = m // 2
    copies = 15 + 3 * (hm - 1)

    def vmem(*shape, dtype=BF16):
        return pltpu.VMEM(shape, dtype)

    grad_a, grad_b = pl.pallas_call(
        functools.partial(kernel, n, m),
        out_shape=[jax.ShapeDtypeStruct((rank, chunk), F32)] * 2,
        in_specs=[pl.BlockSpec(memory_space=pltpu.HBM)] * 12,
        out_specs=[pl.BlockSpec(memory_space=pltpu.VMEM)] * 2,
        scratch_shapes=[
            vmem(2, rows, width),
            vmem(2, rows, width),
            vmem(2, rows, width),
            vmem(rows, width),
            vmem(2, rank, width),
            vmem(2, rank, width),
            vmem(2, 2, rank, width // 2),
            vmem(2, rows, width),
            vmem(2, rows, 128),
            vmem(2, rows, 128),
            vmem(2, rows, 128, dtype=F32),
            vmem(2, rows, 128, dtype=F32),
            vmem(3, 2, hm, 2, rank, chunk),
            vmem(3, hm, 2, rank, chunk),
            vmem(3, hm, 2, rank, chunk),
            vmem(3, hm - 1, 2, rank, chunk),
            vmem(2, rank, chunk),
            vmem(2, rank, chunk),
            vmem(2, rank, chunk),
            vmem(2, rank, chunk),
            pltpu.SemaphoreType.DMA((12,)),
            pltpu.SemaphoreType.DMA((copies,)),
            pltpu.SemaphoreType.DMA((copies,)),
        ],
        compiler_params=pltpu.CompilerParams(
            collective_id=0, has_side_effects=True, vmem_limit_bytes=60 * 2**20
        ),
        name="relay_backward",
    )(*flat)
    return grad_a.T[None], grad_b[None]


def solution(mesh):
    n, m = mesh.shape["pipe"], mesh.shape["dp"]
    row, part = P("pipe", "dp", None), P("dp", None)
    table = P("pipe", None, None)
    return jax.shard_map(
        functools.partial(per_device, n, m),
        mesh=mesh,
        in_specs=(row,) * 6 + (part,) * 2 + (table,) * 4,
        out_specs=(P("pipe", "dp", None), P("pipe", None, "dp")),
        check_vma=False,
    )
```

time: 68.3 us -> 44.8 us (0.66)
  local copies, waits for them, and re-layouts: 14.4 us -> 2.34 us
  Pallas kernels: 52.7 us -> 41.7 us
    unnamed x26 -> x4, local copies, waits for them, and re-layouts: 14.4 us -> 2.34 us
    pallas_call x1, Pallas kernels: 52.7 us -> 41.7 us  [per_device(): pl.pallas_call(functools.partial(kernel, n, m), out_shape=[jax.ShapeDtype...]
where the time goes in v2:
time: 44.8 us; the launch traced here: 44.7 us
  Pallas kernels  41.7 us (93%)
  local copies, waits for them, and re-layouts  2.34 us (5%)
  between operations  0.65 us (1%)
    pallas_call x1, Pallas kernels, per_device(): pl.pallas_call(functools.partial(kernel, n, m), out_shape=[jax.ShapeDtype...  41.7 us
    unnamed x4, local copies, waits for them, and re-layouts  2.34 us

profile of v2, /device:TPU:16, one launch (start us, length us, event | category | flops | bytes accessed | tf_op | source)
XLA Modules:
  0.0 44.7 jit_solution(13752792147797929284)
XLA Ops:
  0.6 41.7 %relay_backward.1 = (f32[32,1536]{1,0:T(8,128)}, f32[32,1536]{1,0:T(8,128)}) custom-call(bf16[64,6144]{1,0:T(8,128)(2,1)} %bitcast.18, bf16[64,6144]{1,0:T(8,128)(2,1)} %bitcast.19, bf16[64,6144]{1,0:T(8,128)(2,1)} %bitcast.20, bf16[64,6144]{1,0:T(8,128)(2,1)} %bitcast.21, bf16[64,6144]{1,0:T(8,128)(2,1)} %bitcast.22, bf16[64,6144]{1,0:T(8,128)(2,1)} %bitcast.23, ...), custom_call_target="tpu_custom_call" | custom-call | tf_op jit(solution)/shard_map/relay_backward/pallas_call | solution.py:381
  42.3 0.0 copy-start
  42.3 1.7 %copy.16 = f32[1,1536,32]{1,2,0:T(8,128)} copy(f32[1,1536,32]{1,2,0:T(8,128)} %bitcast.29) | data formatting | bytes 393216
  44.0 0.0 copy-done
  44.0 0.7 %copy.17 = f32[1,32,1536]{2,1,0:T(8,128)} copy(f32[1,32,1536]{2,1,0:T(8,128)S(1)} %bitcast.28) | data formatting | bytes 393216
Async XLA Ops:
  42.3 1.7 %copy-start = (f32[32,1536]{1,0:T(8,128)S(1)}, f32[32,1536]{1,0:T(8,128)}, u32[]{:S(2)}) copy-start(f32[32,1536]{1,0:T(8,128)} %get-tuple-element.5) | copy-start | bytes 589828

commit v3 on v2

--- a/solution.py
+++ b/solution.py
@@ -131,11 +131,6 @@
     mine = pl.ds(pl.multiple_of(par * half, 128), half)
     toward = (ahead, behind)
     back = (behind, ahead)
-    halves = [
-        send(w, src.at[:, mine], nb.at[w, par], toward[w])
-        for w, src in enumerate((sb, mb))
-    ]
-
     for at in range(4, 10):
         loads[at].start()
     edge = (j == 0, j == n - 1)
@@ -160,7 +155,7 @@
     zero_1 = jnp.zeros((rows, 1), F32)
 
     def loop(body, start=0):
-        return lax.fori_loop(0, tiles, body, start, unroll=2)
+        return lax.fori_loop(0, tiles, body, start, unroll=4)
 
     for at in range(4):
         loads[at].wait()
@@ -182,6 +177,11 @@
         pre2.append(pre)
         hs[w] = wide(pre * jax.nn.sigmoid(pre)).astype(BF16)
         hidden_copies.append(send(4 + w, hs.at[w], hr.at[w], toward[w]))
+
+    halves = [
+        send(w, src.at[:, mine], nb.at[w, par], toward[w])
+        for w, src in enumerate((sb, mb))
+    ]
 
     for at in range(4, 10):
         loads[at].wait()
@@ -221,21 +221,21 @@
 
     def send_quarters(g, copy):
         copy.wait_recv()
-        copies = []
-        for q in range(1, hm):
-            k = peer(q)
-            for i in range(2):
+        copies = ([], [])
+        for i in (1, 0):
+            for q in range(1, hm):
+                k = peer(q)
                 total[g, k, i] = (
                     part[g, par, k, i].astype(F32) + other[g, k, i].astype(F32)
                 ).astype(BF16)
-            copies.append(
-                send(
-                    14 + g * (hm - 1) + q,
-                    total.at[g, k],
-                    arrived.at[g, q - 1],
-                    (j, k * 2 + par),
+                copies[i].append(
+                    send(
+                        15 + (g * (hm - 1) + q - 1) * 2 + i,
+                        total.at[g, k, i],
+                        arrived.at[g, q - 1, i],
+                        (j, k * 2 + par),
+                    )
                 )
-            )
         return copies
 
     def final(g, i):
@@ -298,7 +298,6 @@
     for w in both:
         halves[w].wait_recv()
         passed.append(send(2 + w, nb.at[w, par], nb.at[w, par], pair))
-    quarters.append(send_quarters(1, half_second))
 
     for copy in passed:
         copy.wait_recv()
@@ -315,6 +314,7 @@
         gs[w] = wide(gh)
         returned.append(send(6 + w, gs.at[w], gr.at[w], back[w]))
 
+    quarters.append(send_quarters(1, half_second))
     wdp2 = []
     for w in both:
         returned[w].wait_recv()
@@ -336,23 +336,26 @@
 
     quarters.append(send_quarters(2, half_a))
 
-    for copy in quarters[1]:
-        copy.wait_recv()
+    def arrive(g, i):
+        for copy in quarters[g][i]:
+            copy.wait_recv()
+
     rings = []
     for w in (1, 0):
+        arrive(1, w)
         rs[w] = final(1, w).astype(BF16)
         rings.append(send(11 + w, rs.at[w], rr.at[w], back[w]))
-    for copy in quarters[0]:
-        copy.wait_recv()
+    arrive(0, 1)
     rings[0].wait_recv()
     ms[1] = (final(0, 1) + rr[1].astype(F32)).astype(BF16)
     mirror_b = send(14, ms.at[1], mr.at[1], across)
-    for copy in quarters[2]:
-        copy.wait_recv()
+    arrive(2, 1)
     ms[0] = final(2, 1).astype(BF16)
     mirror_a = send(13, ms.at[0], mr.at[0], across)
+    arrive(0, 0)
     rings[1].wait_recv()
     gb[...] = final(0, 0) + rr[0].astype(F32)
+    arrive(2, 0)
     ga[...] = final(2, 0)
     mirror_b.wait_recv()
     gb[...] = (gb[...] + mr[1].astype(F32)) * factor
@@ -360,7 +363,8 @@
     ga[...] = (ga[...] + mr[0].astype(F32)) * factor
 
     started = halves + passed + hidden_copies + returned + rings
-    started += quarters[0] + quarters[1] + quarters[2]
+    for lists in quarters:
+        started += lists[0] + lists[1]
     for copy in started + [half_first, half_second, half_a, mirror_a, mirror_b]:
         copy.wait_send()
 
@@ -373,7 +377,7 @@
     rank = flat[8].shape[0]
     chunk = width // m
     hm = m // 2
-    copies = 15 + 3 * (hm - 1)
+    copies = 15 + 6 * (hm - 1)
 
     def vmem(*shape, dtype=BF16):
         return pltpu.VMEM(shape, dtype)

time: 44.8 us -> 43.4 us (0.969)
  Pallas kernels: 41.7 us -> 40.3 us
    pallas_call x1, Pallas kernels: 41.7 us -> 40.3 us  [per_device(): pl.pallas_call(functools.partial(kernel, n, m), out_shape=[jax.ShapeDtype...]
where the time goes in v3:
time: 43.4 us; the launch traced here: 43.3 us
  Pallas kernels  40.3 us (93%)
  local copies, waits for them, and re-layouts  2.34 us (5%)
  between operations  0.65 us (1%)
    pallas_call x1, Pallas kernels, per_device(): pl.pallas_call(functools.partial(kernel, n, m), out_shape=[jax.ShapeDtype...  40.3 us
    unnamed x4, local copies, waits for them, and re-layouts  2.34 us

profile of v3, /device:TPU:16, one launch (start us, length us, event | category | flops | bytes accessed | tf_op | source)
XLA Modules:
  0.0 43.3 jit_solution(7394235184345901949)
XLA Ops:
  0.6 40.3 %relay_backward.1 = (f32[32,1536]{1,0:T(8,128)}, f32[32,1536]{1,0:T(8,128)}) custom-call(bf16[64,6144]{1,0:T(8,128)(2,1)} %bitcast.18, bf16[64,6144]{1,0:T(8,128)(2,1)} %bitcast.19, bf16[64,6144]{1,0:T(8,128)(2,1)} %bitcast.20, bf16[64,6144]{1,0:T(8,128)(2,1)} %bitcast.21, bf16[64,6144]{1,0:T(8,128)(2,1)} %bitcast.22, bf16[64,6144]{1,0:T(8,128)(2,1)} %bitcast.23, ...), custom_call_target="tpu_custom_call" | custom-call | tf_op jit(solution)/shard_map/relay_backward/pallas_call | solution.py:385
  40.9 0.0 copy-start
  40.9 1.7 %copy.16 = f32[1,1536,32]{1,2,0:T(8,128)} copy(f32[1,1536,32]{1,2,0:T(8,128)} %bitcast.29) | data formatting | bytes 393216
  42.6 0.0 copy-done
  42.6 0.7 %copy.17 = f32[1,32,1536]{2,1,0:T(8,128)} copy(f32[1,32,1536]{2,1,0:T(8,128)S(1)} %bitcast.28) | data formatting | bytes 393216
Async XLA Ops:
  40.9 1.7 %copy-start = (f32[32,1536]{1,0:T(8,128)S(1)}, f32[32,1536]{1,0:T(8,128)}, u32[]{:S(2)}) copy-start(f32[32,1536]{1,0:T(8,128)} %get-tuple-element.5) | copy-start | bytes 589828
